TPU v7x, 32 devices: a whole 2x2x4 slice. The times are simulated.
32 devices in a mesh: blocks: 2 (over y), space: 4 (over z), tm: 2 (over x), span: 2 (over core).
Axes of the slice: x: 2, y: 2, z: 4, core: 2. Of those that a mesh axis runs over, the one named last changes fastest.
Arguments:
- snapshots: float32 [320, 64, 512], P(('blocks', 'tm'), 'space', 'span'), parts along dimension 0, may hold values from -6 to 6
- lagrange_weights: float32 [512, 6], P(('blocks', 'tm')), parts along dimension 0, may hold values from -3 to 3
- source_start: int32 [512], P(('blocks', 'tm')), parts along dimension 0, may hold values from 0 to 156
- band_len: int32 [512], P(('blocks', 'tm')), parts along dimension 0, may hold values from 4 to 6
- band_list: int32 [8], replicated, may hold values from 0 to 15, as said below
- row_metric: float32 [64], P('space'), may hold values from 0.5 to 2
Outputs:
- spectra: float32 [256, 2, 64, 512], P(('blocks', 'space', 'tm'), None, None, 'span'), parts along dimension 0
There are 2 independent parts, one for each index of `blocks`. A program takes and returns all parts, laid end to end along the dimension named above; an argument that names none is the same for every part. Nothing has to cross between parts.
Inputs may be any that keep to these rules, and one draw needn't show every extreme that they name: `band_list`: 8 distinct band numbers.
All inputs are finite; a program needn't handle non-finite values.
Results may differ from a plain program's by a relative error of at most 0.0001.
Values sent between devices are 32-bit elements; how exact they have to be, the bound alone decides.
A program may use at most 64 MiB of HBM per device.

v0:
```python
import math
import jax
import jax.numpy as jnp
from jax import lax
from jax.sharding import PartitionSpec as P

HALO = 16
NT = 256
BW = 8
NL = 8


def extended(cells, sides, width, closed):
    for axis, dim in sides:
        count = lax.axis_size(axis)
        ends = count if closed else count - 1
        head = lax.slice_in_dim(cells, 0, width, axis=dim)
        tail = lax.slice_in_dim(cells, cells.shape[dim] - width, cells.shape[dim], axis=dim)
        cells = jnp.concatenate(
            [
                lax.ppermute(tail, axis, [(i, (i + 1) % count) for i in range(ends)]),
                cells,
                lax.ppermute(head, axis, [((i + 1) % count, i) for i in range(ends)]),
            ],
            axis=dim,
        )
    return cells


def dft_rows(band_list, row_ids, first_sample, count):
    listed_idx = row_ids // 2
    is_imag = row_ids % 2
    band_pos = listed_idx // BW
    matches = band_pos[:, None] == jnp.arange(band_list.shape[0])[None, :]
    band_of = jnp.sum(jnp.where(matches, band_list[None, :], 0), axis=1)
    frequency = band_of * BW + listed_idx % BW
    sample_ids = first_sample + jnp.arange(count)
    phase_idx = frequency[:, None] * sample_ids[None, :] % NT
    angles = 2.0 * math.pi / NT * phase_idx.astype(jnp.float32)
    window = 0.5 - 0.5 * jnp.cos(2.0 * math.pi / NT * sample_ids.astype(jnp.float32))
    weighting = window / math.sqrt(NT)
    waves = jnp.where(is_imag[:, None] == 0, jnp.cos(angles), -jnp.sin(angles))
    return waves * weighting[None, :]


def shards(snapshots, lagrange_weights, source_start, band_len, band_list, row_metric):
    tm_index = lax.axis_index("tm")
    n_tm, n_space = (lax.axis_size("tm"), lax.axis_size("space"))
    steps_dev, rows_dev, span_cells = snapshots.shape
    samples = source_start.shape[0]
    reach = extended(snapshots, (("tm", 0),), HALO, False)
    reach_len = steps_dev + 2 * HALO
    anchor = tm_index * steps_dev - HALO
    slot_ids = jnp.arange(6)
    columns = source_start[:, None] + slot_ids[None, :] - anchor
    active = slot_ids[None, :] < band_len[:, None]
    selected = (columns[:, :, None] == jnp.arange(reach_len)[None, None, :]) & active[:, :, None]
    interp_matrix = jnp.sum(
        jnp.where(selected, lagrange_weights[:, :, None], jnp.float32(0.0)), axis=1
    )
    total_rows = 2 * NL * BW
    own = total_rows // (n_tm * n_space)
    positions = jnp.arange(total_rows).reshape(n_space, n_tm, own).transpose(1, 0, 2).reshape(-1)
    coeffs = dft_rows(band_list, positions, tm_index * samples, samples)
    combined = jnp.dot(coeffs, interp_matrix, precision=lax.Precision.HIGHEST)
    partial = jnp.dot(
        combined, reach.reshape(reach_len, rows_dev * span_cells), precision=lax.Precision.HIGHEST
    )
    summed = lax.psum_scatter(partial, "tm", scatter_dimension=0, tiled=True)
    summed = summed.reshape(n_space * own, rows_dev, span_cells)
    fields = lax.all_to_all(summed, "space", split_axis=0, concat_axis=1, tiled=True)
    metric = lax.all_gather(row_metric, "space", tiled=True)
    row_padded = jnp.pad(fields, ((0, 0), (1, 1), (0, 0)))
    along_rows = 0.5 * metric[None, :, None] * (row_padded[:, 2:, :] - row_padded[:, :-2, :])
    span_padded = extended(fields, (("span", 2),), 1, True)
    along_span = 0.5 * (span_padded[:, :, 2:] - span_padded[:, :, :-2])
    return jnp.stack((along_rows, along_span), axis=1)


def solution(mesh):
    placed = (
        P(("blocks", "tm"), "space", "span"),
        P(("blocks", "tm"), None),
        P(("blocks", "tm")),
        P(("blocks", "tm")),
        P(),
        P("space"),
    )
    return jax.shard_map(
        shards,
        mesh=mesh,
        in_specs=placed,
        out_specs=P(("blocks", "space", "tm"), None, None, "span"),
        check_vma=False,
    )
```

profile of v0, /device:TPU:0, one launch (start us, length us, event | category | flops | bytes accessed | tf_op | source)
XLA Modules:
  0.0 104.5 jit_solution(15764756894311047526)
XLA Ops:
  6.5 1.2 %fusion.34 = (f32[16,16,256]{2,1,0:T(8,128)S(1)}, f32[16,16,256]{2,1,0:T(8,128)S(1)}) fusion(f32[80,16,256]{2,1,0:T(8,128)} %param.6), kind=kLoop, calls=%fused_computation.64 | loop fusion | bytes 1048576 | tf_op jit(solution)/shard_map/slice | solution.py:18
  7.7 4.9 %collective-permute-start = (f32[16,16,256]{2,1,0:T(8,128)S(1)}, f32[16,16,256]{2,1,0:T(8,128)S(1)}, u32[]{:S(2)}, u32[]{:S(2)}) collective-permute-start(f32[16,16,256]{2,1,0:T(8,128)S(1)} %get-tuple-element.7), channel_id=1, source_target_pairs={{0,2},{1,3},{4,6},{5,7},{8,10},{9,11},{12,14},{13,15},{16,18},{17,... | collective-permute-start | bytes 786440 | tf_op jit(solution)/shard_map/ppermute | solution.py:21
  12.6 1.3 %collective-permute-start.1 = (f32[16,16,256]{2,1,0:T(8,128)S(1)}, f32[16,16,256]{2,1,0:T(8,128)S(1)}, u32[]{:S(2)}, u32[]{:S(2)}) collective-permute-start(f32[16,16,256]{2,1,0:T(8,128)S(1)} %get-tuple-element.8), channel_id=1, source_target_pairs={{2,0},{3,1},{6,4},{7,5},{10,8},{11,9},{14,12},{15,13},{18,16},{19,... | collective-permute-start | bytes 786440 | tf_op jit(solution)/shard_map/ppermute | solution.py:23
  13.9 0.1 reshape.208
  14.0 0.7 iota_compare_fusion.1
  14.7 0.7 add_subtract_fusion
  15.3 0.7 select_reduce_fusion.1
  16.1 0.8 select_reduce_fusion
  16.9 0.1 subtract_multiply_fusion
  16.9 0.5 fusion.10
  17.5 0.6 collective-permute-done
  18.1 4.1 %collective-permute-done.1 = f32[16,16,256]{2,1,0:T(8,128)S(1)} collective-permute-done((f32[16,16,256]{2,1,0:T(8,128)S(1)}, f32[16,16,256]{2,1,0:T(8,128)S(1)}, u32[]{:S(2)}, u32[]{:S(2)}) %collective-permute-start.1) | collective-permute-done | bytes 262176 | tf_op jit(solution)/shard_map/ppermute | solution.py:23
  22.2 0.1 pad_maximum_fusion.1
  22.4 1.4 %copy.12 = f32[14,8,16,256]{3,1,2,0:T(8,128)S(1)} copy(f32[14,8,16,256]{3,2,1,0:T(8,128)S(1)} %bitcast.20) | data formatting | bytes 3670016
  23.8 3.2 %fusion.36 = f32[128,4096]{1,0:T(8,128)} fusion(f32[128,112]{1,0:T(8,128)S(1)} %fusion.10, f32[112,4096]{1,0:T(8,128)S(1)} %bitcast.21), kind=kOutput, calls=%fused_computation.66 | convolution fusion | flops 704643072 | bytes 3989504 | tf_op jit(solution)/shard_map/dot_general | solution.py:66
  26.9 0.0 reduce-scatter.2.cloned.1.call-update
  27.0 32.3 %reduce-scatter.2.cloned.1.call-done = f32[64,4096]{1,0:T(8,128)} async-done(((f32[128,4096]{1,0:T(8,128)}), f32[64,4096]{1,0:T(8,128)}) %reduce-scatter.2.cloned.1.call-update) | async-done | bytes 1048592 | tf_op jit(solution)/shard_map/reduce_scatter | solution.py:69
  59.3 2.5 %copy.13 = f32[8,8,16,256]{3,2,1,0:T(8,128)} copy(f32[8,8,16,256]{3,1,2,0:T(8,128)} %bitcast.23) | data formatting | bytes 2097152
  61.8 4.6 %all-to-all-start = ((f32[64,16,256]{2,1,0:T(8,128)}), f32[64,16,256]{2,1,0:T(8,128)S(1)}, u32[]{:S(2)}, u32[]{:S(2)}) async-start(f32[64,16,256]{2,1,0:T(8,128)} %bitcast.12), calls=%async_computation.1 | async-start | bytes 2097152 | tf_op jit(solution)/shard_map/all_to_all | solution.py:71
  66.4 0.0 copy-done.2
  66.4 0.6 dynamic-slice
  67.6 0.2 dynamic-update-slice
  67.8 21.8 %all-reduce.1 = f32[64]{0:T(128)S(1)} all-reduce(f32[64]{0:T(128)S(1)} %dynamic-update-slice), channel_id=1, replica_groups=mesh['blocks'=2,'space'=4,'tm'=2,'span'=2] {'space'}, use_global_device_ids=true, to_apply=%add.1 | all-reduce | flops 64 | bytes 512
  89.6 2.7 %all-to-all-done = f32[64,16,256]{2,1,0:T(8,128)S(1)} async-done(((f32[64,16,256]{2,1,0:T(8,128)}), f32[64,16,256]{2,1,0:T(8,128)S(1)}, u32[]{:S(2)}, u32[]{:S(2)}) %all-to-all-start) | async-done | bytes 1048608 | tf_op jit(solution)/shard_map/all_to_all | solution.py:71
  92.3 0.1 copy.10
  92.4 0.2 fusion.35
  92.6 0.1 collective-permute-start.2
  92.7 0.5 collective-permute-start.3
  93.2 1.4 %collective-permute-done.2 = f32[16,64,1]{2,1,0:T(8,128)S(1)} collective-permute-done((f32[16,64,1]{2,1,0:T(8,128)S(1)}, f32[16,64,1]{2,1,0:T(8,128)S(1)}, u32[]{:S(2)}, u32[]{:S(2)}) %collective-permute-start.2) | collective-permute-done | bytes 4128 | tf_op jit(solution)/shard_map/ppermute | solution.py:23
  94.6 0.7 collective-permute-done.3
  95.4 0.8 fusion.2
  96.2 1.5 %pad_maximum_fusion = f32[16,2,64,256]{3,2,1,0:T(8,128)} fusion(f32[16,1,64,256]{3,2,1,0:T(8,128)S(1)} %get-tuple-element.10, f32[16,1,64,256]{3,2,1,0:T(8,128)S(1)} %get-tuple-element.9), kind=kLoop, calls=%fused_computation | loop fusion | flops 524288 | bytes 4194304 | tf_op jit(solution)/shard_map/stack | solution.py:77
  (12 shorter events, 0.1 us)
Async XLA Ops:
  6.5 15.7 %copy-start = (f32[80,16,256]{2,1,0:T(8,128)S(1)}, f32[80,16,256]{2,1,0:T(8,128)}, u32[]{:S(2)}) copy-start(f32[80,16,256]{2,1,0:T(8,128)} %param.6) | copy-start | bytes 3932164
  6.5 52.7 %reduce-scatter.2.cloned.1.call-start = ((), (), s32[]{:S(2)}) async-start(), calls=%async_computation.2 | async-start | bytes 3145728 | tf_op jit(solution)/shard_map/reduce_scatter | solution.py:69
  7.7 10.4 %collective-permute-start = (f32[16,16,256]{2,1,0:T(8,128)S(1)}, f32[16,16,256]{2,1,0:T(8,128)S(1)}, u32[]{:S(2)}, u32[]{:S(2)}) collective-permute-start(f32[16,16,256]{2,1,0:T(8,128)S(1)} %get-tuple-element.7), channel_id=1, source_target_pairs={{0,2},{1,3},{4,6},{5,7},{8,10},{9,11},{12,14},{13,15},{16,18},{17,... | collective-permute-start | bytes 786440 | tf_op jit(solution)/shard_map/ppermute | solution.py:21
  12.6 9.7 %collective-permute-start.1 = (f32[16,16,256]{2,1,0:T(8,128)S(1)}, f32[16,16,256]{2,1,0:T(8,128)S(1)}, u32[]{:S(2)}, u32[]{:S(2)}) collective-permute-start(f32[16,16,256]{2,1,0:T(8,128)S(1)} %get-tuple-element.8), channel_id=1, source_target_pairs={{2,0},{3,1},{6,4},{7,5},{10,8},{11,9},{14,12},{15,13},{18,16},{19,... | collective-permute-start | bytes 786440 | tf_op jit(solution)/shard_map/ppermute | solution.py:23
  59.3 7.1 %copy-start.2 = (u32[32]{0:T(128)S(1)}, u32[32]{0:T(128)}, u32[]{:S(2)}) copy-start(u32[32]{0:T(128)} %constant.95) | copy-start | bytes 388
  59.3 8.3 %copy-start.1 = (f32[16]{0:T(128)S(1)}, f32[16]{0:T(128)}, u32[]{:S(2)}) copy-start(f32[16]{0:T(128)} %param.11) | copy-start | bytes 196
  61.8 30.5 %all-to-all-start = ((f32[64,16,256]{2,1,0:T(8,128)}), f32[64,16,256]{2,1,0:T(8,128)S(1)}, u32[]{:S(2)}, u32[]{:S(2)}) async-start(f32[64,16,256]{2,1,0:T(8,128)} %bitcast.12), calls=%async_computation.1 | async-start | bytes 2097152 | tf_op jit(solution)/shard_map/all_to_all | solution.py:71
  92.6 2.0 %collective-permute-start.2 = (f32[16,64,1]{2,1,0:T(8,128)S(1)}, f32[16,64,1]{2,1,0:T(8,128)S(1)}, u32[]{:S(2)}, u32[]{:S(2)}) collective-permute-start(f32[16,64,1]{2,1,0:T(8,128)S(1)} %get-tuple-element.11), channel_id=1, source_target_pairs={{1,0},{0,1},{3,2},{2,3},{5,4},{4,5},{7,6},{6,7},{9,8},{8,9},{11,10... | collective-permute-start | bytes 12296 | tf_op jit(solution)/shard_map/ppermute | solution.py:23
  92.7 2.6 %collective-permute-start.3 = (f32[16,64,1]{2,1,0:T(8,128)S(1)}, f32[16,64,1]{2,1,0:T(8,128)S(1)}, u32[]{:S(2)}, u32[]{:S(2)}) collective-permute-start(f32[16,64,1]{2,1,0:T(8,128)S(1)} %get-tuple-element.12), channel_id=1, source_target_pairs={{0,1},{1,0},{2,3},{3,2},{4,5},{5,4},{6,7},{7,6},{8,9},{9,8},{10,11... | collective-permute-start | bytes 12296 | tf_op jit(solution)/shard_map/ppermute | solution.py:21
Sparse Core Ops, SparseCore 0:
  27.1 32.1 reduce-scatter.1
where the time goes:
time: 105 us
  waiting for transfers between devices  42 us (40%)
  blocking collectives  21.8 us (21%)
  between operations  14.1 us (13%)
  starting transfers between devices  11.3 us (11%)
  local copies, waits for them, and re-layouts  6.28 us (6%)
  other arithmetic  5.39 us (5%)
  matrix products  3.72 us (4%)
    reduce_scatter x1, waiting for transfers between devices, shards(): summed = lax.psum_scatter(partial, 'tm', scatter_dimension=0, tiled=True)  32.3 us
    unnamed x1, blocking collectives  21.8 us
    ppermute x2, waiting for transfers between devices, extended(): lax.ppermute(head, axis, [((i + 1) % count, i) for i in range(ends)])  5.52 us
    ppermute x2, starting transfers between devices, extended(): lax.ppermute(tail, axis, [(i, (i + 1) % count) for i in range(ends)])  5.36 us
    unnamed x11, local copies, waits for them, and re-layouts  4.74 us
    all_to_all x1, starting transfers between devices, shards(): lax.all_to_all(summed, 'space', split_axis=0, concat_axis=1, tiled=True)  4.59 us
    dot_general x1, matrix products, shards(): jnp.dot(combined, reach.reshape(reach_len, rows_dev * span_cells), precis...  3.18 us
    all_to_all x1, waiting for transfers between devices, shards(): lax.all_to_all(summed, 'space', split_axis=0, concat_axis=1, tiled=True)  2.73 us
  transfers between devices with their start and end apart: 6, of which 6 were waited for; matrix products, arithmetic and copies ran while one was open for 4% of the time, Pallas kernels for 0%

commit v1 on v0

--- a/solution.py
+++ b/solution.py
@@ -8,6 +8,32 @@
 NT = 256
 BW = 8
 NL = 8
+
+
+def indices_note(here_x, axis_no, local_block):
+    right_arr, seen_now = (here_x.shape[:axis_no], here_x.shape[axis_no + 1 :])
+    return jnp.moveaxis(here_x.reshape(*right_arr, local_block, -1, *seen_now), axis_no, 0)
+
+
+def values_step_on(local, at_axis):
+    base_arr = list(local.shape[1:])
+    base_arr[at_axis] *= local.shape[0]
+    return jnp.moveaxis(local, 0, at_axis).reshape(base_arr)
+
+
+def _extend_terms(array_in, peer_axis, sheet, payload):
+    state_next, y_new = (lax.psum(1, peer_axis), lax.axis_index(peer_axis))
+    m_next = indices_note(array_in, sheet, state_next)
+    slots = [m_next[y_new]]
+    for jj in range(1, state_next):
+        h_now = m_next[(y_new + jj) % state_next]
+        slots.append(
+            lax.ppermute(
+                h_now, peer_axis, [(pp, (pp + jj) % state_next) for pp in range(state_next)]
+            )
+        )
+    m_next = jnp.stack(slots, 0)[(y_new - jnp.arange(state_next)) % state_next]
+    return values_step_on(m_next, payload)
 
 
 def extended(cells, sides, width, closed):
@@ -68,7 +94,7 @@
     )
     summed = lax.psum_scatter(partial, "tm", scatter_dimension=0, tiled=True)
     summed = summed.reshape(n_space * own, rows_dev, span_cells)
-    fields = lax.all_to_all(summed, "space", split_axis=0, concat_axis=1, tiled=True)
+    fields = _extend_terms(summed, "space", 0, 1)
     metric = lax.all_gather(row_metric, "space", tiled=True)
     row_padded = jnp.pad(fields, ((0, 0), (1, 1), (0, 0)))
     along_rows = 0.5 * metric[None, :, None] * (row_padded[:, 2:, :] - row_padded[:, :-2, :])

time: 105 us -> 101 us (0.962)
  waiting for transfers between devices: 42 us -> 39.2 us
  blocking collectives: 21.8 us -> 20.4 us
    all_to_all x1 -> x0, starting transfers between devices: 4.59 us -> none  [shards(): lax.all_to_all(summed, 'space', split_axis=0, concat_axis=1, tiled=True)]
    ppermute x0 -> x3, starting transfers between devices: none -> 4.47 us  [_extend_terms(): lax.ppermute(h_now, peer_axis, [(pp, (pp + jj) % state_next) for pp in ra...]
    all_to_all x1 -> x0, waiting for transfers between devices: 2.73 us -> none  [shards(): lax.all_to_all(summed, 'space', split_axis=0, concat_axis=1, tiled=True)]
    unnamed x1, blocking collectives: 21.8 us -> 20.4 us
  transfers between devices with their start and end apart: 6 -> 8, of which waited for: 6 -> 5; matrix products, arithmetic and copies ran while one was open for 4% -> 4% of each run, Pallas kernels for 0% -> 0%
where the time goes in v1:
time: 101 us; the launch traced here: 100 us
  waiting for transfers between devices  39.2 us (39%)
  blocking collectives  20.4 us (20%)
  between operations  14.3 us (14%)
  starting transfers between devices  11.2 us (11%)
  local copies, waits for them, and re-layouts  6.03 us (6%)
  other arithmetic  5.48 us (5%)
  matrix products  3.72 us (4%)
    reduce_scatter x1, waiting for transfers between devices, shards(): summed = lax.psum_scatter(partial, 'tm', scatter_dimension=0, tiled=True)  32.3 us
    unnamed x1, blocking collectives  20.4 us
    ppermute x2, waiting for transfers between devices, extended(): lax.ppermute(head, axis, [((i + 1) % count, i) for i in range(ends)])  5.52 us
    ppermute x2, starting transfers between devices, extended(): lax.ppermute(tail, axis, [(i, (i + 1) % count) for i in range(ends)])  5.36 us
    ppermute x3, starting transfers between devices, _extend_terms(): lax.ppermute(h_now, peer_axis, [(pp, (pp + jj) % state_next) for pp in ra...  4.47 us
    unnamed x11, local copies, waits for them, and re-layouts  3.77 us
    dot_general x1, matrix products, shards(): jnp.dot(combined, reach.reshape(reach_len, rows_dev * span_cells), precis...  3.18 us
    another operation x2, other arithmetic, shards(): return jnp.stack((along_rows, along_span), axis=1)  2.32 us
  transfers between devices with their start and end apart: 8, of which 5 were waited for; matrix products, arithmetic and copies ran while one was open for 4% of the time, Pallas kernels for 0%

profile of v1, /device:TPU:0, one launch (start us, length us, event | category | flops | bytes accessed | tf_op | source)
XLA Modules:
  0.0 100.3 jit_solution(2345763963756720093)
XLA Ops:
  6.5 1.2 %fusion.36 = (f32[16,16,256]{2,1,0:T(8,128)S(1)}, f32[16,16,256]{2,1,0:T(8,128)S(1)}) fusion(f32[80,16,256]{2,1,0:T(8,128)} %param.6), kind=kLoop, calls=%fused_computation.77 | loop fusion | bytes 1048576 | tf_op jit(solution)/shard_map/slice | solution.py:44
  7.7 4.9 %collective-permute-start = (f32[16,16,256]{2,1,0:T(8,128)S(1)}, f32[16,16,256]{2,1,0:T(8,128)S(1)}, u32[]{:S(2)}, u32[]{:S(2)}) collective-permute-start(f32[16,16,256]{2,1,0:T(8,128)S(1)} %get-tuple-element.7), channel_id=1, source_target_pairs={{0,2},{1,3},{4,6},{5,7},{8,10},{9,11},{12,14},{13,15},{16,18},{17,... | collective-permute-start | bytes 786440 | tf_op jit(solution)/shard_map/ppermute | solution.py:47
  12.6 1.3 %collective-permute-start.1 = (f32[16,16,256]{2,1,0:T(8,128)S(1)}, f32[16,16,256]{2,1,0:T(8,128)S(1)}, u32[]{:S(2)}, u32[]{:S(2)}) collective-permute-start(f32[16,16,256]{2,1,0:T(8,128)S(1)} %get-tuple-element.8), channel_id=1, source_target_pairs={{2,0},{3,1},{6,4},{7,5},{10,8},{11,9},{14,12},{15,13},{18,16},{19,... | collective-permute-start | bytes 786440 | tf_op jit(solution)/shard_map/ppermute | solution.py:49
  13.9 0.1 reshape.257
  14.0 0.7 iota_compare_fusion.1
  14.7 0.7 add_subtract_fusion
  15.3 0.7 select_reduce_fusion.1
  16.1 0.8 select_reduce_fusion
  16.9 0.5 fusion.10
  17.5 0.6 collective-permute-done
  18.1 4.1 %collective-permute-done.1 = f32[16,16,256]{2,1,0:T(8,128)S(1)} collective-permute-done((f32[16,16,256]{2,1,0:T(8,128)S(1)}, f32[16,16,256]{2,1,0:T(8,128)S(1)}, u32[]{:S(2)}, u32[]{:S(2)}) %collective-permute-start.1) | collective-permute-done | bytes 262176 | tf_op jit(solution)/shard_map/ppermute | solution.py:49
  22.2 0.1 pad_maximum_fusion.1
  22.4 1.4 %copy.12 = f32[14,8,16,256]{3,1,2,0:T(8,128)S(1)} copy(f32[14,8,16,256]{3,2,1,0:T(8,128)S(1)} %bitcast.30) | data formatting | bytes 3670016
  23.8 3.2 %fusion.38 = f32[128,4096]{1,0:T(8,128)} fusion(f32[128,112]{1,0:T(8,128)S(1)} %fusion.10, f32[112,4096]{1,0:T(8,128)S(1)} %bitcast.31), kind=kOutput, calls=%fused_computation.79 | convolution fusion | flops 704643072 | bytes 3989504 | tf_op jit(solution)/shard_map/dot_general | solution.py:92
  27.0 32.3 %reduce-scatter.2.cloned.1.call-done = f32[64,4096]{1,0:T(8,128)} async-done(((f32[128,4096]{1,0:T(8,128)}), f32[64,4096]{1,0:T(8,128)}) %reduce-scatter.2.cloned.1.call-update) | async-done | bytes 1048592 | tf_op jit(solution)/shard_map/reduce_scatter | solution.py:95
  59.3 1.6 %copy.13 = f32[8,8,16,256]{3,2,1,0:T(8,128)S(1)} copy(f32[8,8,16,256]{3,1,2,0:T(8,128)} %bitcast.34) | data formatting | bytes 2097152
  60.9 0.1 constant_dynamic-slice_fusion
  61.0 3.4 %collective-permute-start.4 = (f32[16,16,256]{2,1,0:T(8,128)S(1)}, f32[16,16,256]{2,1,0:T(8,128)S(1)}, u32[]{:S(2)}, u32[]{:S(2)}) collective-permute-start(f32[16,16,256]{2,1,0:T(8,128)S(1)} %get-tuple-element.14), channel_id=1, source_target_pairs={{0,12},{4,0},{8,4},{12,8},{1,13},{5,1},{9,5},{13,9},{2,14},{6,2},{... | collective-permute-start | bytes 786440 | tf_op jit(solution)/shard_map/ppermute | solution.py:31
  64.3 1.1 %collective-permute-start.2 = (f32[16,16,256]{2,1,0:T(8,128)S(1)}, f32[16,16,256]{2,1,0:T(8,128)S(1)}, u32[]{:S(2)}, u32[]{:S(2)}) collective-permute-start(f32[16,16,256]{2,1,0:T(8,128)S(1)} %get-tuple-element.16), channel_id=1, source_target_pairs={{0,4},{4,8},{8,12},{12,0},{1,5},{5,9},{9,13},{13,1},{2,6},{6,10},{... | collective-permute-start | bytes 786440 | tf_op jit(solution)/shard_map/ppermute | solution.py:31
  65.4 0.6 dynamic-slice
  66.7 0.2 dynamic-update-slice
  66.9 20.4 %all-reduce.1 = f32[64]{0:T(128)S(1)} all-reduce(f32[64]{0:T(128)S(1)} %dynamic-update-slice), channel_id=1, replica_groups=mesh['blocks'=2,'space'=4,'tm'=2,'span'=2] {'space'}, use_global_device_ids=true, to_apply=%add.1 | all-reduce | flops 64 | bytes 512
  87.4 0.1 pad_maximum_fusion.4
  87.5 0.6 gather_fusion
  88.1 0.1 copy.10
  88.2 0.2 fusion.37
  88.4 0.1 collective-permute-start.5
  88.5 0.5 collective-permute-start.6
  89.0 1.4 %collective-permute-done.5 = f32[16,64,1]{2,1,0:T(8,128)S(1)} collective-permute-done((f32[16,64,1]{2,1,0:T(8,128)S(1)}, f32[16,64,1]{2,1,0:T(8,128)S(1)}, u32[]{:S(2)}, u32[]{:S(2)}) %collective-permute-start.5) | collective-permute-done | bytes 4128 | tf_op jit(solution)/shard_map/ppermute | solution.py:49
  90.4 0.7 collective-permute-done.6
  91.1 0.8 fusion.2
  92.0 1.5 %pad_maximum_fusion = f32[16,2,64,256]{3,2,1,0:T(8,128)} fusion(f32[16,1,64,256]{3,2,1,0:T(8,128)S(1)} %get-tuple-element.10, f32[16,1,64,256]{3,2,1,0:T(8,128)S(1)} %get-tuple-element.9), kind=kLoop, calls=%fused_computation.1 | loop fusion | flops 524288 | bytes 4194304 | tf_op jit(solution)/shard_map/stack | solution.py:103
  (21 shorter events, 0.2 us)
Async XLA Ops:
  6.5 15.7 %copy-start = (f32[80,16,256]{2,1,0:T(8,128)S(1)}, f32[80,16,256]{2,1,0:T(8,128)}, u32[]{:S(2)}) copy-start(f32[80,16,256]{2,1,0:T(8,128)} %param.6) | copy-start | bytes 3932164
  6.5 52.7 %reduce-scatter.2.cloned.1.call-start = ((), (), s32[]{:S(2)}) async-start(), calls=%async_computation.1 | async-start | bytes 3145728 | tf_op jit(solution)/shard_map/reduce_scatter | solution.py:95
  7.7 10.4 %collective-permute-start = (f32[16,16,256]{2,1,0:T(8,128)S(1)}, f32[16,16,256]{2,1,0:T(8,128)S(1)}, u32[]{:S(2)}, u32[]{:S(2)}) collective-permute-start(f32[16,16,256]{2,1,0:T(8,128)S(1)} %get-tuple-element.7), channel_id=1, source_target_pairs={{0,2},{1,3},{4,6},{5,7},{8,10},{9,11},{12,14},{13,15},{16,18},{17,... | collective-permute-start | bytes 786440 | tf_op jit(solution)/shard_map/ppermute | solution.py:47
  12.6 9.7 %collective-permute-start.1 = (f32[16,16,256]{2,1,0:T(8,128)S(1)}, f32[16,16,256]{2,1,0:T(8,128)S(1)}, u32[]{:S(2)}, u32[]{:S(2)}) collective-permute-start(f32[16,16,256]{2,1,0:T(8,128)S(1)} %get-tuple-element.8), channel_id=1, source_target_pairs={{2,0},{3,1},{6,4},{7,5},{10,8},{11,9},{14,12},{15,13},{18,16},{19,... | collective-permute-start | bytes 786440 | tf_op jit(solution)/shard_map/ppermute | solution.py:49
  59.3 6.2 %copy-start.2 = (u32[32]{0:T(128)S(1)}, u32[32]{0:T(128)}, u32[]{:S(2)}) copy-start(u32[32]{0:T(128)} %constant.131) | copy-start | bytes 388
  59.3 7.4 %copy-start.1 = (f32[16]{0:T(128)S(1)}, f32[16]{0:T(128)}, u32[]{:S(2)}) copy-start(f32[16]{0:T(128)} %param.11) | copy-start | bytes 196
  61.0 26.4 %collective-permute-start.4 = (f32[16,16,256]{2,1,0:T(8,128)S(1)}, f32[16,16,256]{2,1,0:T(8,128)S(1)}, u32[]{:S(2)}, u32[]{:S(2)}) collective-permute-start(f32[16,16,256]{2,1,0:T(8,128)S(1)} %get-tuple-element.14), channel_id=1, source_target_pairs={{0,12},{4,0},{8,4},{12,8},{1,13},{5,1},{9,5},{13,9},{2,14},{6,2},{... | collective-permute-start | bytes 786440 | tf_op jit(solution)/shard_map/ppermute | solution.py:31
  64.3 23.1 %collective-permute-start.3 = (f32[16,16,256]{2,1,0:T(8,128)S(1)}, f32[16,16,256]{2,1,0:T(8,128)S(1)}, u32[]{:S(2)}, u32[]{:S(2)}) collective-permute-start(f32[16,16,256]{2,1,0:T(8,128)S(1)} %get-tuple-element.15), channel_id=1, source_target_pairs={{0,8},{4,12},{8,0},{12,4},{1,9},{5,13},{9,1},{13,5},{2,10},{6,14},... | collective-permute-start | bytes 786440 | tf_op jit(solution)/shard_map/ppermute | solution.py:31
  64.3 23.1 %collective-permute-start.2 = (f32[16,16,256]{2,1,0:T(8,128)S(1)}, f32[16,16,256]{2,1,0:T(8,128)S(1)}, u32[]{:S(2)}, u32[]{:S(2)}) collective-permute-start(f32[16,16,256]{2,1,0:T(8,128)S(1)} %get-tuple-element.16), channel_id=1, source_target_pairs={{0,4},{4,8},{8,12},{12,0},{1,5},{5,9},{9,13},{13,1},{2,6},{6,10},{... | collective-permute-start | bytes 786440 | tf_op jit(solution)/shard_map/ppermute | solution.py:31
  88.4 2.0 %collective-permute-start.5 = (f32[16,64,1]{2,1,0:T(8,128)S(1)}, f32[16,64,1]{2,1,0:T(8,128)S(1)}, u32[]{:S(2)}, u32[]{:S(2)}) collective-permute-start(f32[16,64,1]{2,1,0:T(8,128)S(1)} %get-tuple-element.11), channel_id=1, source_target_pairs={{1,0},{0,1},{3,2},{2,3},{5,4},{4,5},{7,6},{6,7},{9,8},{8,9},{11,10... | collective-permute-start | bytes 12296 | tf_op jit(solution)/shard_map/ppermute | solution.py:49
  88.5 2.6 %collective-permute-start.6 = (f32[16,64,1]{2,1,0:T(8,128)S(1)}, f32[16,64,1]{2,1,0:T(8,128)S(1)}, u32[]{:S(2)}, u32[]{:S(2)}) collective-permute-start(f32[16,64,1]{2,1,0:T(8,128)S(1)} %get-tuple-element.12), channel_id=1, source_target_pairs={{0,1},{1,0},{2,3},{3,2},{4,5},{5,4},{6,7},{7,6},{8,9},{9,8},{10,11... | collective-permute-start | bytes 12296 | tf_op jit(solution)/shard_map/ppermute | solution.py:47
Sparse Core Ops, SparseCore 0:
  27.1 32.1 reduce-scatter.1
